TPU v7x, 32 devices: a whole 2x2x4 slice. The times are simulated.
32 devices in a mesh: dp: 8 (over z, x), tensor: 4 (over y, core).
Axes of the slice: x: 2, y: 2, z: 4, core: 2. Of those that a mesh axis runs over, the one named last changes fastest.
Arguments:
- hidden_in: bfloat16 [16, 512, 768], P('dp', 'tensor'), may hold values from -6 to 6
- lengths: int32 [16], P('dp'), may hold values from 32 to 512, as said below
- w_query: bfloat16 [768, 768], P(None, 'tensor'), may hold values from -0.21875 to 0.21875
- b_query: float32 [768], P('tensor'), may hold values from -3 to 3
- w_key: bfloat16 [768, 768], P(None, 'tensor'), may hold values from -0.21875 to 0.21875
- w_value: bfloat16 [768, 768], P(None, 'tensor'), may hold values from -0.21875 to 0.21875
- b_value: float32 [768], P('tensor'), may hold values from -3 to 3
- w_out: bfloat16 [768, 768], P('tensor'), may hold values from -0.875 to 0.875
- b_out: float32 [768], replicated, may hold values from -3 to 3
- norm1_gain: float32 [768], replicated, may hold values from 0.5 to 1.5
- norm1_shift: float32 [768], replicated, may hold values from -3 to 3
- w_up: bfloat16 [768, 3072], P(None, 'tensor'), may hold values from -0.21875 to 0.21875
- b_up: float32 [3072], P('tensor'), may hold values from -3 to 3
- w_down: bfloat16 [3072, 768], P('tensor'), may hold values from -0.21875 to 0.21875
- b_down: float32 [768], replicated, may hold values from -3 to 3
- norm2_gain: float32 [768], replicated, may hold values from 0.5 to 1.5
- norm2_shift: float32 [768], replicated, may hold values from -3 to 3
- out_grad: float32 [16, 512, 768], P('dp', 'tensor'), may hold values from -6 to 6
Outputs:
- out: float32 [16, 512, 768], P('dp', 'tensor')
- grad_input: float32 [16, 512, 768], P('dp', 'tensor')
- grad_w_query: float32 [768, 768], P(None, 'tensor')
- grad_b_query: float32 [768], P('tensor')
- grad_w_key: float32 [768, 768], P(None, 'tensor')
- grad_w_value: float32 [768, 768], P(None, 'tensor')
- grad_b_value: float32 [768], P('tensor')
- grad_w_out: float32 [768, 768], P('tensor')
- grad_b_out: float32 [768], replicated
- grad_norm1_gain: float32 [768], replicated
- grad_norm1_shift: float32 [768], replicated
- grad_w_up: float32 [768, 3072], P(None, 'tensor')
- grad_b_up: float32 [3072], P('tensor')
- grad_w_down: float32 [3072, 768], P('tensor')
- grad_b_down: float32 [768], replicated
- grad_norm2_gain: float32 [768], replicated
- grad_norm2_shift: float32 [768], replicated
Inputs may be any that keep to these rules, and one draw needn't show every extreme that they name: `lengths`: in each aligned block of 2 rows, one row, which one drawn from the seed, has length 512; the others are skewed short.
All inputs are finite; a program needn't handle non-finite values.
Results may differ from a plain program's by a relative error of at most 0.035.
Values may be sent and summed in bfloat16 or wider, within the bound.
A program may use at most 128 MiB of HBM per device.

v0:
```python
import functools

import jax
import jax.numpy as jnp
from jax import lax
from jax.experimental import pallas as pl
from jax.experimental.pallas import tpu as pltpu
from jax.sharding import PartitionSpec as P

HEAD = 64
NORM_EPS = 1e-12
NEG = -1000000000.0
GELU_C = 0.7978845608
GELU_A = 0.044715

NN = (((1,), (0,)), ((), ()))
NT = (((1,), (1,)), ((), ()))
TN = (((0,), (0,)), ((), ()))

b16 = jnp.bfloat16
f32 = jnp.float32


def dot(left, right, dims):
    return lax.dot_general(left, right, dims, preferred_element_type=f32)


def rms_back(dout, scaled, rstd, gain):
    dscaled = dout * gain
    return rstd * (
        dscaled
        - jnp.mean(dscaled, axis=-1, keepdims=True)
        - scaled * jnp.mean(dscaled * scaled, axis=-1, keepdims=True)
    )


def col_sum(value):
    return jnp.sum(value, axis=0, keepdims=True)


def whole_step(
    cfg,
    len_ref,
    hid,
    og,
    wq,
    wk,
    wv,
    wo,
    wu,
    wd,
    bu,
    bq,
    bv,
    b_out,
    gain1,
    shift1,
    b_down,
    gain2,
    shift2,
    out,
    gib_out,
    gq_out,
    gk_out,
    gv_out,
    go_out,
    gu_out,
    gd_out,
    sm_out,
    w,
    hb,
    qkv,
    ex,
    inv,
    ctx,
    zs,
    rs,
    yb,
    act,
    gp,
    X,
    Y,
    dffn,
    dpre,
    dattn,
    dqkv,
    dct,
    xs,
    xr,
    bur,
    bqr,
    bvr,
    bcol,
    acc,
    sm,
    smr,
    G,
    gs,
    yr,
    xh,
    zr,
    hr,
    F,
    lsem,
    fs,
    fr,
    wys,
    wyr,
    wxs,
    wxr,
    wzs,
    wzr,
    wfs,
    wfr,
    es,
    er,
    ys,
    yrs,
    gxs,
    gxr,
    zss,
    zrs,
    hss,
    hrs,
    azs,
    azr,
    axs,
    axr,
    os,
    sms,
    smrs,
):
    T, D, A, B, C, R, NP, NH = (
        cfg["T"],
        cfg["D"],
        cfg["A"],
        cfg["B"],
        cfg["C"],
        cfg["R"],
        cfg["NP"],
        cfg["NH"],
    )
    NCH = T // C
    W = C
    TOT = 4 * A + 2 * D
    NS = TOT // R
    HR = R // 2
    Q = HR // NP
    NHH = A // HEAD
    HEADS = 2 * NHH
    MESH = pl.DeviceIdType.MESH
    UP, DN = 4 * A, 4 * A + D

    d = lax.axis_index("dp")
    t = lax.axis_index("tensor")
    y = t // 2
    c = t % 2
    x = d % 2
    z = d // 2
    zlo = z % NP
    zhi = z // NP
    t2 = (t + 2) % 4
    sib = (d, t + 1 - 2 * c)
    par = (d, t2)
    xp = (d + 1 - 2 * x, t)

    def zdev(k):
        return ((zhi * NP + (zlo + k) % NP) * 2 + x, t)

    def hdev(k):
        return ((((zhi + k) % NH) * NP + zlo) * 2 + x, t)

    def remote(src, dst, send, recv, dev):
        return pltpu.make_async_remote_copy(
            src_ref=src,
            dst_ref=dst,
            send_sem=send,
            recv_sem=recv,
            device_id=dev,
            device_id_type=MESH,
        )

    local = [
        pltpu.make_async_copy(hid.at[y], hb.at[0, pl.ds(t * B, B)], lsem.at[0]),
        pltpu.make_async_copy(wo, w.at[0, pl.ds(3 * A, A)], lsem.at[1]),
        pltpu.make_async_copy(wu, w.at[0, pl.ds(UP, D)], lsem.at[2]),
        pltpu.make_async_copy(wd, w.at[0, pl.ds(DN, D)], lsem.at[3]),
        pltpu.make_async_copy(og.at[0], Y.at[pl.ds(0, B)], lsem.at[4]),
        pltpu.make_async_copy(og.at[1], Y.at[pl.ds(B, B)], lsem.at[5]),
        pltpu.make_async_copy(wq, w.at[0, pl.ds(0, A)], lsem.at[6]),
        pltpu.make_async_copy(wk, w.at[0, pl.ds(A, A)], lsem.at[7]),
        pltpu.make_async_copy(wv, w.at[0, pl.ds(2 * A, A)], lsem.at[8]),
    ]
    for copy in local:
        copy.start()

    barrier = pltpu.get_barrier_semaphore()
    friends = [sib, par, xp] + [zdev(k) for k in range(1, NP)] + [hdev(k) for k in range(1, NH)]
    for dev in friends:
        pl.semaphore_signal(barrier, inc=1, device_id=dev, device_id_type=MESH)
    pl.semaphore_wait(barrier, len(friends))

    hid_sib = remote(hid.at[y], hb.at[0, pl.ds(t * B, B)], fs.at[0], fr.at[0], sib)
    hid_par = remote(hid.at[1 - y], hb.at[0, pl.ds(t * B, B)], fs.at[1], fr.at[1], par)
    bias_par = [
        remote(mine, theirs, fs.at[9 + i], fr.at[9 + i], par)
        for i, (mine, theirs) in enumerate(((bu, bur), (bq, bqr), (bv, bvr)))
    ]
    hid_sib.start()

    acc[...] = jnp.zeros_like(acc)

    WST = TOT // A
    WCH = A // 4
    zb = z % 2
    zp = ((z + 1 - 2 * zb) * 2 + x, t)

    def wrows(i, qx, qz):
        return pl.ds(pl.multiple_of(i * A + (2 * qx + qz) * WCH, WCH), WCH)

    def wy(i):
        rows = wrows(i, x, zb)
        return remote(w.at[0, rows], w.at[1, rows], wys.at[i], wyr.at[i], par)

    def wx(i):
        rows = wrows(i, x, zb)
        return remote(w.at[1, rows], w.at[1, rows], wxs.at[i], wxr.at[i], xp)

    def wz(i):
        rows = wrows(i, x, zb)
        return remote(w.at[1, rows], w.at[1, rows], wzs.at[i], wzr.at[i], zp)

    def wf(i):
        rows = wrows(i, 1 - x, zb) if i % 2 == 0 else wrows(i, x, 1 - zb)
        return remote(w.at[1, rows], w.at[1, rows], wfs.at[i], wfr.at[i], zp if i % 2 == 0 else xp)

    LOOK = 3

    def pump(i):
        wy(i).wait_recv()
        wx(i).start()
        wz(i).start()
        if i + LOOK < WST:
            wy(i + LOOK).start()

    def pass_on(i):
        (wx if i % 2 == 0 else wz)(i).wait_recv()
        wf(i).start()

    def have(lo, hi):
        for i in range(lo, hi):
            (wz if i % 2 == 0 else wx)(i).wait_recv()
            wf(i).wait_recv()

    for copy in local[6:]:
        copy.wait()
    wy(0).start()
    hid_par.start()
    for copy in bias_par:
        copy.start()
    wy(1).start()
    wy(2).start()
    for copy in local[:6]:
        copy.wait()
    G[0 : 2 * B] = Y[0 : 2 * B].astype(b16)

    pump(0)
    hid_par.wait_recv()
    rows_t2 = pl.ds(t2 * B, B)
    hid_fwd = remote(hb.at[0, rows_t2], hb.at[0, rows_t2], fs.at[3], fr.at[3], sib)
    hid_fwd.start()
    for copy in bias_par:
        copy.wait_recv()
    for half, sources in enumerate(((bq, bv), (bqr, bvr))):
        for i, source in enumerate(sources):
            bcol[half, i * A : (i + 1) * A] = jnp.transpose(jnp.broadcast_to(source[...], (128, A)))
    hid_sib.wait_recv()
    hid_fwd.wait_recv()

    b_out, gain1, shift1, b_down, gain2, shift2 = (
        ref[...].reshape(1, D) for ref in (b_out, gain1, shift1, b_down, gain2, shift2)
    )
    length = len_ref[y]

    def loop(lo, hi, f):
        def step(i, carry):
            f(i)
            return carry

        lax.fori_loop(lo, hi, step, 0)

    def chunk(m):
        return pl.ds(pl.multiple_of(m * C, C), C)

    def wide_chunk(m):
        return pl.ds(pl.multiple_of(m * W, W), W)

    def xcopy(k, m):
        return remote(xs.at[k % 2, chunk(m)], xr.at[k % 2, chunk(m)], es.at[k % 2, m], er.at[k % 2, m], sib)

    def xsend(k, m, value):
        xs[k % 2, chunk(m)] = value.astype(b16)
        xcopy(k, m).start()

    def xget(k, m):
        xcopy(k, m).wait()
        return xs[k % 2, chunk(m)].astype(f32) + xr[k % 2, chunk(m)].astype(f32)

    def project(l, m):
        tok = wide_chunk(m)
        for half in range(2):
            got = dot(w[half, 0 : 3 * A], hb[l, tok], NT)
            base = half * 3 * A
            bq = jnp.concatenate([bcol[half, 0:A]] * (W // 128), axis=1)
            bv = jnp.concatenate([bcol[half, A : 2 * A]] * (W // 128), axis=1)
            qkv[l, base : base + A, tok] = ((got[0:A] + bq).astype(b16) * b16(HEAD**-0.5)).astype(b16)
            qkv[l, base + A : base + 2 * A, tok] = got[A : 2 * A].astype(b16)
            qkv[l, base + 2 * A : base + 3 * A, tok] = (got[2 * A : 3 * A] + bv).astype(b16)

    def head_rows(h, part):
        base = (h // NHH) * (3 * A) + part * A + (h % NHH) * HEAD
        return pl.ds(pl.multiple_of(base, HEAD), HEAD)

    def attend(l, h):
        counted = lax.broadcasted_iota(jnp.int32, (T, T), 0) < length
        scores = dot(qkv[l, head_rows(h, 1)], qkv[l, head_rows(h, 0)], TN)
        scores = jnp.where(counted, scores, NEG)
        top = jnp.max(scores, axis=0, keepdims=True)
        e = jnp.exp(scores - top)
        one = 1.0 / jnp.sum(e, axis=0, keepdims=True)
        eb = e.astype(b16)
        ex[l, h] = eb
        inv[l, h] = one
        got = dot(qkv[l, head_rows(h, 2)], eb, NN) * one
        ctx[l, pl.ds(pl.multiple_of(h * HEAD, HEAD), HEAD)] = got.astype(b16)

    def attend_range(l, lo, hi):
        loop(lo, hi, lambda h: attend(l, h))

    def attn_out(l, k):
        def step(m):
            tok = chunk(m)
            part = dot(ctx[l, 0:A, tok], w[0, 3 * A : 4 * A], TN)
            part += dot(ctx[l, A : 2 * A, tok], w[1, 3 * A : 4 * A], TN)
            xsend(k, m, part)

        loop(0, NCH, step)

    def zrows(z_at, m):
        return pl.ds(pl.multiple_of(z_at * T + m * C, C), C)

    def norm(resid, gain, shift, z_at, m):
        rows = chunk(m)
        centre = resid - jnp.mean(resid, axis=-1, keepdims=True)
        rstd = lax.rsqrt(jnp.mean(centre * centre, axis=-1, keepdims=True) + NORM_EPS)
        scaled = centre * rstd
        zs[zrows(z_at, m)] = scaled.astype(b16)
        rs[rows, z_at : z_at + 1] = rstd
        return scaled * gain + shift

    def norm_one(l, k, m):
        rows = chunk(m)
        before = hb[0, rows].astype(f32) if l == 0 else X[rows]
        first = norm(xget(k, m) + b_out + before, gain1, shift1, 2 * l, m)
        Y[rows] = first
        yb[l, rows] = first.astype(b16)

    def up_chunk(l, m):
        rows = chunk(m)
        for half, source in enumerate((bu, bur)):
            cols = pl.ds(half * D, D)
            pre = dot(yb[l, rows], w[half, UP : UP + D], NN) + source[...].reshape(1, D)
            square = pre * pre
            th = jnp.tanh(GELU_C * pre * (1.0 + GELU_A * square))
            more = 0.5 * (1.0 + th)
            act[l, rows, cols] = (pre * more).astype(b16)
            slope = more + (0.5 * GELU_C) * pre * (1.0 - th * th) * (1.0 + (3 * GELU_A) * square)
            gp[l, rows, cols] = slope.astype(b16)

    def down_chunk(l, k, m):
        rows = chunk(m)
        part = dot(act[l, rows, 0:D], w[0, DN : DN + D], NN)
        part += dot(act[l, rows, D : 2 * D], w[1, DN : DN + D], NN)
        xsend(k, m, part)

    def norm_two(l, k, m):
        rows = chunk(m)
        result = norm(xget(k, m) + b_down + Y[rows], gain2, shift2, 2 * l + 1, m)
        X[rows] = result
        if l == 0:
            hb[1, rows] = result.astype(b16)

    pump(1)
    pass_on(0)
    pump(2)
    pass_on(1)
    pump(3)
    pass_on(2)
    have(0, 3)
    loop(0, T // W, lambda m: project(0, m))
    done = 4
    for h in range(HEADS):
        attend(0, h)
        if done < WST:
            pump(done)
            pass_on(done - 1)
            done += 1
    have(3, 4)
    attn_out(0, 0)
    while done < WST:
        pump(done)
        pass_on(done - 1)
        done += 1
    pass_on(WST - 1)
    loop(0, NCH, lambda m: norm_one(0, 0, m))
    have(4, 8)
    loop(0, NCH, lambda m: up_chunk(0, m))
    og_rows = pl.ds(t * B, B)
    og_mine, og_other = G.at[pl.ds(y * B, B)], G.at[pl.ds((1 - y) * B, B)]
    og_keep = pltpu.make_async_copy(og_mine, dattn.at[0, og_rows], lsem.at[0])
    og_sib = remote(og_mine, dattn.at[0, og_rows], fs.at[4], fr.at[4], sib)
    og_par = remote(og_other, dattn.at[0, og_rows], fs.at[5], fr.at[5], par)
    og_keep.start()
    og_par.start()
    og_sib.start()
    have(8, WST)
    loop(0, NCH, lambda m: down_chunk(0, 1, m))

    def next_layer(m):
        norm_two(0, 1, m)
        project(1, m)

    loop(0, T // W, next_layer)

    attend_range(1, 0, HEADS)
    og_par.wait_recv()
    og_fwd = remote(dattn.at[0, rows_t2], dattn.at[0, rows_t2], fs.at[6], fr.at[6], sib)
    og_fwd.start()
    attn_out(1, 2)

    def feed_forward(m):
        norm_one(1, 2, m)
        up_chunk(1, m)
        down_chunk(1, 3, m)

    loop(0, NCH, feed_forward)
    loop(0, NCH, lambda m: norm_two(1, 3, m))
    out_keep = pltpu.make_async_copy(X.at[pl.ds(t * B, B)], out.at[y], lsem.at[1])
    out_par = remote(X.at[pl.ds(t2 * B, B)], out.at[y], fs.at[7], fr.at[7], par)
    out_keep.start()
    out_par.start()
    og_keep.wait()
    og_sib.wait_recv()
    og_fwd.wait_recv()

    def ffn_back(l, k, m):
        rows = chunk(m)
        dout = dattn[0, rows].astype(f32) if l == 1 else X[rows]
        scaled = zs[zrows(2 * l + 1, m)].astype(f32)
        dr = rms_back(dout, scaled, rs[rows, 2 * l + 1 : 2 * l + 2], gain2)
        acc[3:4] += col_sum(dr)
        acc[4:5] += col_sum(dout * scaled)
        acc[5:6] += col_sum(dout)
        Y[rows] = dr
        drb = dr.astype(b16)
        dffn[l, rows] = drb
        part = None
        for half in range(2):
            cols = pl.ds(half * D, D)
            dact = dot(drb, w[half, DN : DN + D], NT)
            dp = (dact * gp[l, rows, cols].astype(f32)).astype(b16)
            dpre[l, rows, cols] = dp
            row = 6 + 8 * half
            acc[row : row + 1] += col_sum(dp.astype(f32))
            got = dot(dp, w[half, UP : UP + D], NT)
            part = got if part is None else part + got
        xsend(k, m, part)

    def attn_out_back(l, k, m):
        rows = chunk(m)
        dfirst = Y[rows] + xget(k, m)
        scaled = zs[zrows(2 * l, m)].astype(f32)
        dr = rms_back(dfirst, scaled, rs[rows, 2 * l : 2 * l + 1], gain1)
        acc[0:1] += col_sum(dr)
        acc[1:2] += col_sum(dfirst * scaled)
        acc[2:3] += col_sum(dfirst)
        Y[rows] = dr
        drb = dr.astype(b16)
        dattn[l, rows] = drb

    def context_back(l):
        for half in range(2):
            got = dot(w[half, 3 * A : 4 * A], dattn[l], NT)
            for j in range(NHH):
                h = half * NHH + j
                scaled_rows = got[j * HEAD : (j + 1) * HEAD] * inv[l, h]
                dct[h * HEAD : (h + 1) * HEAD] = scaled_rows.astype(b16)

    def attend_back(l, h):
        mine = pl.ds(pl.multiple_of(h * HEAD, HEAD), HEAD)
        dc = dct[mine]
        dprobs = dot(qkv[l, head_rows(h, 2)], dc, TN)
        eb = ex[l, h]
        ef = eb.astype(f32)
        inner = col_sum(ef * dprobs) * inv[l, h]
        ds = (ef * (dprobs - inner)).astype(b16)
        dqkv[l, head_rows(h, 2)] = dot(dc, eb, NT).astype(b16)
        dqkv[l, head_rows(h, 0)] = (dot(qkv[l, head_rows(h, 1)], ds, NN) * (HEAD**-0.5)).astype(b16)
        dqkv[l, head_rows(h, 1)] = dot(qkv[l, head_rows(h, 0)], ds, NT).astype(b16)

    def attend_back_range(l, lo, hi):
        loop(lo, hi, lambda h: attend_back(l, h))

    def project_back(l, k):
        def step(m):
            tok = chunk(m)
            part = dot(dqkv[l, 0 : 3 * A, tok], w[0, 0 : 3 * A], TN)
            part += dot(dqkv[l, 3 * A : 6 * A, tok], w[1, 0 : 3 * A], TN)
            xsend(k, m, part)

        loop(0, NCH, step)
        ones = jnp.ones((8, T), b16)
        for half in range(2):
            sums = dot(ones, dqkv[l, half * 3 * A : (half + 1) * 3 * A], NT)
            row = 7 + 8 * half
            acc[row : row + 1, 0 : 3 * A] += sums[0:1]

    loop(0, NCH, lambda m: ffn_back(1, 4, m))
    loop(0, NCH, lambda m: attn_out_back(1, 4, m))
    context_back(1)
    attend_back_range(1, 0, HEADS)
    for copy in (og_sib, og_par, og_fwd):
        copy.wait_send()
    out_keep.wait()
    out_par.wait_send()
    project_back(1, 5)

    def first_layer(m):
        rows = chunk(m)
        X[rows] = Y[rows] + xget(5, m)
        ffn_back(0, 6, m)

    loop(0, NCH, first_layer)

    def both(ref, cols=slice(None)):
        value = ref[:, :, cols]
        return value.reshape(2 * value.shape[1], value.shape[2])

    FREE = T - 4 * A

    def grad_down(half, dst, off=0):
        dy = both(dffn)
        for i in reversed(range(D // 256)):
            left = both(act, slice(half * D + i * 256, half * D + (i + 1) * 256))
            dst[off + DN + i * 256 : off + DN + (i + 1) * 256] = dot(left, dy, TN).astype(b16)

    def grad_up(half, dst, off=0):
        dy = both(dpre, slice(half * D, (half + 1) * D))
        for i in reversed(range(D // 256)):
            left = both(yb, slice(i * 256, (i + 1) * 256))
            dst[off + UP + i * 256 : off + UP + (i + 1) * 256] = dot(left, dy, TN).astype(b16)

    def grad_attn(half, dst):
        rows = slice(half * A, (half + 1) * A)
        got = dot(ctx[0, rows], dattn[0], NN) + dot(ctx[1, rows], dattn[1], NN)
        dst[3 * A : 4 * A] = got.astype(b16)
        rows = slice(half * 3 * A, (half + 1) * 3 * A)
        got = dot(dqkv[0, rows], hb[0], NN) + dot(dqkv[1, rows], hb[1], NN)
        dst[0 : 3 * A] = got.astype(b16)

    def top_of(s):
        return pl.multiple_of(TOT - (s + 1) * R, R)

    def piece(s):
        return pl.ds(top_of(s), R)

    def half_of(s, which):
        return pl.ds(pl.multiple_of(top_of(s) + which * HR, HR), HR)

    def part_of(s, which, p):
        return pl.ds(pl.multiple_of(top_of(s) + which * HR + p * Q, Q), Q)

    def ycopy_ffn(s):
        src = zs.at[pl.ds(pl.multiple_of(top_of(s) + FREE, R), R)]
        return remote(src, yr.at[piece(s)], ys.at[s], yrs.at[s], par)

    def ycopy_attn(s):
        return remote(gs.at[piece(s)], yr.at[piece(s)], ys.at[s], yrs.at[s], par)

    def ycopy(s):
        return remote(yr.at[piece(s)], yr.at[piece(s)], ys.at[s], yrs.at[s], par)

    def gxcopy(s):
        return remote(G.at[half_of(s, 1 - x)], xh.at[s], gxs.at[s], gxr.at[s], xp)

    def zcopy(s, k):
        src = G.at[part_of(s, x, (zlo + k) % NP)]
        return remote(src, zr.at[s, k - 1], zss.at[s, k - 1], zrs.at[s, k - 1], zdev(k))

    def hcopy(s, k):
        src = G.at[part_of(s, x, zlo)]
        return remote(src, hr.at[s % 2, k - 1], hss.at[s, k - 1], hrs.at[s, k - 1], hdev(k))

    def azcopy(s, k):
        rows = part_of(s, x, zlo)
        return remote(F.at[rows], F.at[rows], azs.at[s, k - 1], azr.at[s, k - 1], zdev(k))

    def axcopy(s, k):
        rows = part_of(s, x, (zlo + NP - k) % NP)
        return remote(F.at[rows], F.at[rows], axs.at[s, k], axr.at[s, k], xp)

    ocopies = [
        pltpu.make_async_copy(F.at[pl.ds(lo, rows)], ref, os.at[i])
        for i, (ref, lo, rows) in enumerate(
            (
                (gd_out, DN, D),
                (gu_out, UP, D),
                (go_out, 3 * A, A),
                (gv_out, 2 * A, A),
                (gk_out, A, A),
                (gq_out, 0, A),
            )
        )
    ]

    YLOOK = 3

    def ystart(s):
        if isinstance(s, int):
            if s < NS:
                (ycopy_ffn if s < 2 * D // R else ycopy_attn)(s).start()
            return

        @pl.when(s < 2 * D // R)
        def _():
            ycopy_ffn(s).start()

        @pl.when((s >= 2 * D // R) & (s < NS))
        def _():
            ycopy_attn(s).start()

    def stage_x(s):
        ycopy(s).wait_recv()
        ystart(s + YLOOK)
        for which in (1 - x, x):
            rows = half_of(s, which)
            G[rows] = (G[rows].astype(f32) + yr[rows].astype(f32)).astype(b16)
            if which is not x:
                gxcopy(s).start()

    def stage_z(s):
        gxcopy(s).wait_recv()
        rows = half_of(s, x)
        G[rows] = (G[rows].astype(f32) + xh[s].astype(f32)).astype(b16)
        for k in range(1, NP):
            zcopy(s, k).start()

    def stage_sum(s):
        rows = part_of(s, x, zlo)
        total = G[rows].astype(f32)
        for k in range(1, NP):
            zcopy(s, k).wait_recv()
            total += zr[s, k - 1].astype(f32)
        if NH > 1:
            G[rows] = total.astype(b16)
            for k in range(1, NH):
                hcopy(s, k).start()
            for k in range(1, NH):
                hcopy(s, k).wait()
                total += hr[s % 2, k - 1].astype(f32)
        F[rows] = total.astype(b16)
        for k in range(1, NP):
            azcopy(s, k).start()
        axcopy(s, 0).start()

    def stage_swap(s):
        for k in range(1, NP):
            azcopy(s, k).wait_recv()
            axcopy(s, k).start()

    def stage_out(s):
        for k in range(NP):
            axcopy(s, k).wait_recv()

    stages = (stage_x, stage_z, stage_sum, stage_swap, stage_out)

    def run(i):
        for lag, stage in enumerate(stages):
            s = i - lag
            if isinstance(s, int) and not 0 <= s < NS:
                continue
            stage(s)

    grad_down(1, zs, FREE)
    for s in range(YLOOK):
        ystart(s)
    grad_up(1, zs, FREE)
    grad_down(0, G)
    loop(0, NCH, lambda m: attn_out_back(0, 6, m))
    context_back(0)
    run(0)
    grad_up(0, G)
    attend_back_range(0, 0, HEADS // 2)
    run(1)
    attend_back_range(0, HEADS // 2, HEADS)
    run(2)
    project_back(0, 7)
    grad_attn(1, gs)
    run(3)
    acc[8:14] = acc[0:6]
    sm_y = remote(acc.at[pl.ds(8, 8)], smr.at[0], sms.at[0], smrs.at[0], par)
    sm_y.start()

    def last(m):
        rows = chunk(m)
        X[rows] = Y[rows] + xget(7, m)

    loop(0, NCH, last)
    xs[0, 0:B] = X[pl.ds(t * B, B)].astype(b16)
    xs[0, B : 2 * B] = X[pl.ds(t2 * B, B)].astype(b16)
    gi_keep = pltpu.make_async_copy(xs.at[0, pl.ds(0, B)], gib_out.at[y], lsem.at[2])
    gi_par = remote(xs.at[0, pl.ds(B, B)], gib_out.at[y], fs.at[8], fr.at[8], par)
    gi_keep.start()
    gi_par.start()
    grad_attn(0, G)

    loop(4, D // R + 4, run)
    ocopies[0].start()
    loop(D // R + 4, NS, run)
    for i in range(NS, NS + 2):
        run(i)
    sm_y.wait_recv()
    sm[0] = acc[0:8] + smr[0]
    sm_x = remote(sm.at[0], smr.at[1], sms.at[1], smrs.at[1], xp)
    sm_x.start()
    run(NS + 2)
    sm_x.wait_recv()
    sm[1] = sm[0] + smr[1]
    sm_z = [
        remote(sm.at[1], smr.at[1 + k], sms.at[1 + k], smrs.at[1 + k], zdev(k)) for k in range(1, NP)
    ]
    for copy in sm_z:
        copy.start()
    run(NS + 3)
    for copy in ocopies[1:]:
        copy.start()
    total = sm[1]
    for k, copy in enumerate(sm_z):
        copy.wait_recv()
        total += smr[2 + k]
    sm[2] = total
    if NH > 1:
        sm_h = [
            remote(sm.at[2], smr.at[NP + k], sms.at[NP + k], smrs.at[NP + k], hdev(k))
            for k in range(1, NH)
        ]
        for copy in sm_h:
            copy.start()
        for k, copy in enumerate(sm_h):
            copy.wait()
            total += smr[NP + 1 + k]
    sm_out[...] = total

    for copy in (hid_sib, hid_par, *bias_par, hid_fwd, gi_par, sm_y, sm_x):
        copy.wait_send()
    for copy in sm_z:
        copy.wait_send()
    out_par.wait_recv()
    gi_par.wait_recv()
    gi_keep.wait()
    for i in range(WST):
        wy(i).wait_send()
        wx(i).wait_send()
        wz(i).wait_send()
        wf(i).wait_send()

    def drain(s):
        ycopy(s).wait_send()
        gxcopy(s).wait_send()
        for k in range(1, NP):
            zcopy(s, k).wait_send()
            azcopy(s, k).wait_send()
        for k in range(NP):
            axcopy(s, k).wait_send()

    loop(0, NS, drain)
    for copy in ocopies:
        copy.wait()


def widen(*refs):
    names = 7
    big, result, small = refs[:names], refs[names], refs[names + 1]
    refs = refs[names + 2 :]
    wide, result_out, vectors = refs[:names], refs[names], refs[names + 1 : names + 10]
    refs = refs[names + 10 :]
    narrow, broad = refs[:names], refs[names : 2 * names]
    through, isem, osem = refs[2 * names :]
    loads = [pltpu.make_async_copy(big[i], narrow[i], isem.at[i]) for i in range(names)]
    stores = [pltpu.make_async_copy(broad[i], wide[i], osem.at[i]) for i in range(names)]
    keep_in = pltpu.make_async_copy(result, through, isem.at[names])
    keep = pltpu.make_async_copy(through, result_out, osem.at[names])
    for copy in loads:
        copy.start()
    keep_in.start()
    for i, ref in enumerate(vectors):
        if i < 7:
            ref[...] = small[i, :]
        else:
            rows = ref.shape[0]
            at = (i - 7) * 2 * rows
            ref[...] = small[7, at : at + rows]
    for load, store, i in zip(loads, stores, range(names)):
        load.wait()
        broad[i][...] = narrow[i][...].astype(f32)
        store.start()
    keep_in.wait()
    keep.start()
    for copy in stores:
        copy.wait()
    keep.wait()


def shards(
    dp,
    hidden_in,
    lengths,
    w_query,
    b_query,
    w_key,
    w_value,
    b_value,
    w_out,
    b_out,
    norm1_gain,
    norm1_shift,
    w_up,
    b_up,
    w_down,
    b_down,
    norm2_gain,
    norm2_shift,
    out_grad,
):
    _, B, D = hidden_in.shape
    A = w_query.shape[1]
    T = 4 * B
    TOT = 4 * A + 2 * D
    R = 128
    HR = R // 2
    nz = dp // 2
    NP = 1
    while nz % (2 * NP) == 0 and HR % (32 * NP) == 0:
        NP *= 2
    NH = nz // NP
    C = T // 2
    NCH = T // C
    NS = TOT // R
    Q = HR // NP
    heads = 2 * A // HEAD
    cfg = dict(T=T, D=D, A=A, B=B, C=C, R=R, NP=NP, NH=NH)
    rows = [
        value if value.shape[0] == D else value.reshape(1, -1)
        for value in (
            b_up,
            b_query,
            b_value,
            b_out,
            norm1_gain,
            norm1_shift,
            b_down,
            norm2_gain,
            norm2_shift,
        )
    ]
    V = functools.partial(pltpu.VMEM)
    DMA = pltpu.SemaphoreType.DMA
    NPx = max(NP - 1, 1)
    NHx = max(NH - 1, 1)
    scratch = [
        V((2, TOT, D), b16),
        V((2, T, D), b16),
        V((2, 6 * A, T), b16),
        V((2, heads, T, T), b16),
        V((2, heads, 1, T), f32),
        V((2, 2 * A, T), b16),
        V((max(4 * T, T + 2 * D), D), b16),
        V((T, 128), f32),
        V((2, T, D), b16),
        V((2, T, 2 * D), b16),
        V((2, T, 2 * D), b16),
        V((T, D), f32),
        V((T, D), f32),
        V((2, T, D), b16),
        V((2, T, 2 * D), b16),
        V((2, T, D), b16),
        V((2, 6 * A, T), b16),
        V((2 * A, T), b16),
        V((2, T, D), b16),
        V((2, T, D), b16),
        V((D,), f32),
        V((1, A), f32),
        V((1, A), f32),
        V((2, 2 * A, 128), f32),
        V((16, D), f32),
        V((3, 8, D), f32),
        V((NP + NH, 8, D), f32),
        V((TOT, D), b16),
        V((4 * A, D), b16),
        V((TOT, D), b16),
        V((NS, HR, D), b16),
        V((NS, NPx, Q, D), b16),
        V((2, NHx, Q, D), b16),
        V((TOT, D), b16),
        DMA((9,)),
        DMA((12,)),
        DMA((12,)),
        DMA((TOT // A,)),
        DMA((TOT // A,)),
        DMA((TOT // A,)),
        DMA((TOT // A,)),
        DMA((TOT // A,)),
        DMA((TOT // A,)),
        DMA((TOT // A,)),
        DMA((TOT // A,)),
        DMA((2, NCH)),
        DMA((2, NCH)),
        DMA((NS,)),
        DMA((NS,)),
        DMA((NS,)),
        DMA((NS,)),
        DMA((NS, NPx)),
        DMA((NS, NPx)),
        DMA((NS, NHx)),
        DMA((NS, NHx)),
        DMA((NS, NPx)),
        DMA((NS, NPx)),
        DMA((NS, NP)),
        DMA((NS, NP)),
        DMA((6,)),
        DMA((NP + NH,)),
        DMA((NP + NH,)),
    ]
    anywhere = pl.BlockSpec(memory_space=pl.ANY)
    vmem = pl.BlockSpec(memory_space=pltpu.VMEM)
    smem = pl.BlockSpec(memory_space=pltpu.SMEM)
    result, gib, gq, gk, gv, go, gu, gd, small = pl.pallas_call(
        functools.partial(whole_step, cfg),
        out_shape=(
            jax.ShapeDtypeStruct((2, B, D), f32),
            jax.ShapeDtypeStruct((2, B, D), b16),
            jax.ShapeDtypeStruct((A, D), b16),
            jax.ShapeDtypeStruct((A, D), b16),
            jax.ShapeDtypeStruct((A, D), b16),
            jax.ShapeDtypeStruct((A, D), b16),
            jax.ShapeDtypeStruct((D, D), b16),
            jax.ShapeDtypeStruct((D, D), b16),
            jax.ShapeDtypeStruct((8, D), f32),
        ),
        in_specs=[smem] + [anywhere] * 8 + [vmem] * 9,
        out_specs=(anywhere,) * 8 + (vmem,),
        scratch_shapes=scratch,
        compiler_params=pltpu.CompilerParams(
            collective_id=0, has_side_effects=True, vmem_limit_bytes=64 * 2**20
        ),
    )(
        lengths,
        hidden_in,
        out_grad,
        w_query.T,
        w_key.T,
        w_value.T,
        w_out,
        w_up,
        w_down,
        *rows,
    )
    bigs = (gd, gu, go, gq, gk, gv, gib)
    gd, gu, go, gq, gk, gv, gi, result, *vectors = pl.pallas_call(
        widen,
        out_shape=tuple(jax.ShapeDtypeStruct(v.shape, f32) for v in bigs + (result,))
        + (jax.ShapeDtypeStruct((D,), f32),) * 7
        + (jax.ShapeDtypeStruct((A,), f32),) * 2,
        in_specs=[anywhere] * 8 + [vmem],
        out_specs=(anywhere,) * 8 + (vmem,) * 9,
        scratch_shapes=[V(v.shape, b16) for v in bigs]
        + [V(v.shape, f32) for v in bigs]
        + [V(result.shape, f32), DMA((8,)), DMA((8,))],
        compiler_params=pltpu.CompilerParams(vmem_limit_bytes=64 * 2**20),
    )(*bigs, result, small)
    db_out, dgain1, dshift1, db_down, dgain2, dshift2, db_up, db_query, db_value = vectors
    return (
        result,
        gi,
        gq.T,
        db_query,
        gk.T,
        gv.T,
        db_value,
        go,
        db_out,
        dgain1,
        dshift1,
        gu,
        db_up,
        gd,
        db_down,
        dgain2,
        dshift2,
    )


def solution(mesh):
    placed = (
        P("dp", "tensor", None),
        P("dp"),
        P(None, "tensor"),
        P("tensor"),
        P(None, "tensor"),
        P(None, "tensor"),
        P("tensor"),
        P("tensor", None),
        P(),
        P(),
        P(),
        P(None, "tensor"),
        P("tensor"),
        P("tensor", None),
        P(),
        P(),
        P(),
        P("dp", "tensor", None),
    )
    return jax.shard_map(
        functools.partial(shards, mesh.shape["dp"]),
        mesh=mesh,
        in_specs=placed,
        out_specs=(
            P("dp", "tensor", None),
            P("dp", "tensor", None),
            P(None, "tensor"),
            P("tensor"),
            P(None, "tensor"),
            P(None, "tensor"),
            P("tensor"),
            P("tensor", None),
            P(),
            P(),
            P(),
            P(None, "tensor"),
            P("tensor"),
            P("tensor", None),
            P(),
            P(),
            P(),
        ),
        check_vma=False,
    )
```

profile of v0, /device:TPU:0, one launch (start us, length us, event | category | flops | bytes accessed | tf_op | source)
XLA Modules:
  0.0 204.1 jit_solution(15993880374519215950)
XLA Ops:
  0.7 196.9 %shard_map.305 = (f32[2,128,768]{2,1,0:T(8,128)}, bf16[2,128,768]{2,1,0:T(8,128)(2,1)}, bf16[192,768]{1,0:T(8,128)(2,1)}, bf16[192,768]{1,0:T(8,128)(2,1)}, bf16...) custom-call(s32[2]{0:T(128)} %len_ref.1, ...), custom_call_target="tpu_custom_call" | custom-call | tf_op jit(solution)/shard_map/pallas_call | solution.py:947
  197.6 6.3 %shard_map.306 = (f32[768,768]{1,0:T(8,128)}, f32[768,768]{1,0:T(8,128)}, f32[192,768]{1,0:T(8,128)}, f32[192,768]{1,0:T(8,128)}, f32[192,768]{1,0:T(8,128)}, /*...) custom-call(bf16[768,768]{1,0:T(8,128)(2,1)} %get-tuple-element.43.r, ...), custom_call_target="tpu_custom_call" | custom-call | tf_op jit(solution)/shard_map/pallas_call | solution.py:979
where the time goes:
time: 204 us
  Pallas kernels  203 us (100%)
    pallas_call x1, Pallas kernels, shards(): pl.pallas_call(functools.partial(whole_step, cfg), out_shape=(jax.ShapeDt...  197 us
    pallas_call x1, Pallas kernels, shards(): pl.pallas_call(widen, out_shape=tuple((jax.ShapeDtypeStruct(v.shape, f32)...  6.3 us

commit v1 on v0

--- a/solution.py
+++ b/solution.py
@@ -112,6 +112,8 @@
     wzr,
     wfs,
     wfr,
+    wds,
+    wdr,
     es,
     er,
     ys,
@@ -141,7 +143,8 @@
         cfg["NH"],
     )
     NCH = T // C
-    W = C
+    W = 2 * C
+    NW = T // W
     TOT = 4 * A + 2 * D
     NS = TOT // R
     HR = R // 2
@@ -234,14 +237,25 @@
         rows = wrows(i, 1 - x, zb) if i % 2 == 0 else wrows(i, x, 1 - zb)
         return remote(w.at[1, rows], w.at[1, rows], wfs.at[i], wfr.at[i], zp if i % 2 == 0 else xp)
 
-    LOOK = 3
+    LATE = WST - D // A
+
+    def wd(i):
+        rows = wrows(i, 1 - x, 1 - zb)
+        return remote(w.at[0, rows], w.at[1, rows], wds.at[i], wdr.at[i], par)
+
+    LOOK = 4
+
+    def send_quarters(i):
+        if i < WST:
+            wy(i).start()
+            if i >= LATE:
+                wd(i).start()
 
     def pump(i):
         wy(i).wait_recv()
         wx(i).start()
         wz(i).start()
-        if i + LOOK < WST:
-            wy(i + LOOK).start()
+        send_quarters(i + LOOK)
 
     def pass_on(i):
         (wx if i % 2 == 0 else wz)(i).wait_recv()
@@ -249,22 +263,31 @@
 
     def have(lo, hi):
         for i in range(lo, hi):
+            if i >= LATE:
+                wx(i).wait_recv()
+                wz(i).wait_recv()
+                wd(i).wait_recv()
+                continue
             (wz if i % 2 == 0 else wx)(i).wait_recv()
             wf(i).wait_recv()
 
     for copy in local[6:]:
         copy.wait()
-    wy(0).start()
+    for i in range(3):
+        wy(i).start()
     hid_par.start()
     for copy in bias_par:
         copy.start()
-    wy(1).start()
-    wy(2).start()
     for copy in local[:6]:
         copy.wait()
+    wy(3).start()
     G[0 : 2 * B] = Y[0 : 2 * B].astype(b16)
 
     pump(0)
+    pump(1)
+    pass_on(0)
+    pump(2)
+    pass_on(1)
     hid_par.wait_recv()
     rows_t2 = pl.ds(t2 * B, B)
     hid_fwd = remote(hb.at[0, rows_t2], hb.at[0, rows_t2], fs.at[3], fr.at[3], sib)
@@ -305,6 +328,10 @@
     def xget(k, m):
         xcopy(k, m).wait()
         return xs[k % 2, chunk(m)].astype(f32) + xr[k % 2, chunk(m)].astype(f32)
+
+    def xsend_wide(k, m, value):
+        xsend(k, 2 * m, value[0:C])
+        xsend(k, 2 * m + 1, value[C:W])
 
     def project(l, m):
         tok = wide_chunk(m)
@@ -339,12 +366,12 @@
 
     def attn_out(l, k):
         def step(m):
-            tok = chunk(m)
+            tok = wide_chunk(m)
             part = dot(ctx[l, 0:A, tok], w[0, 3 * A : 4 * A], TN)
             part += dot(ctx[l, A : 2 * A, tok], w[1, 3 * A : 4 * A], TN)
-            xsend(k, m, part)
-
-        loop(0, NCH, step)
+            xsend_wide(k, m, part)
+
+        loop(0, NW, step)
 
     def zrows(z_at, m):
         return pl.ds(pl.multiple_of(z_at * T + m * C, C), C)
@@ -366,22 +393,22 @@
         yb[l, rows] = first.astype(b16)
 
     def up_chunk(l, m):
-        rows = chunk(m)
+        rows = wide_chunk(m)
         for half, source in enumerate((bu, bur)):
             cols = pl.ds(half * D, D)
             pre = dot(yb[l, rows], w[half, UP : UP + D], NN) + source[...].reshape(1, D)
             square = pre * pre
-            th = jnp.tanh(GELU_C * pre * (1.0 + GELU_A * square))
-            more = 0.5 * (1.0 + th)
-            act[l, rows, cols] = (pre * more).astype(b16)
-            slope = more + (0.5 * GELU_C) * pre * (1.0 - th * th) * (1.0 + (3 * GELU_A) * square)
+            more = 0.5 + 0.5 * jnp.tanh(pre * (GELU_C + (GELU_C * GELU_A) * square))
+            value = pre * more
+            act[l, rows, cols] = value.astype(b16)
+            slope = more + value * (1.0 - more) * (2.0 * GELU_C + (6.0 * GELU_C * GELU_A) * square)
             gp[l, rows, cols] = slope.astype(b16)
 
     def down_chunk(l, k, m):
-        rows = chunk(m)
+        rows = wide_chunk(m)
         part = dot(act[l, rows, 0:D], w[0, DN : DN + D], NN)
         part += dot(act[l, rows, D : 2 * D], w[1, DN : DN + D], NN)
-        xsend(k, m, part)
+        xsend_wide(k, m, part)
 
     def norm_two(l, k, m):
         rows = chunk(m)
@@ -390,31 +417,33 @@
         if l == 0:
             hb[1, rows] = result.astype(b16)
 
-    pump(1)
-    pass_on(0)
-    pump(2)
-    pass_on(1)
+    pass_on(2)
     pump(3)
-    pass_on(2)
     have(0, 3)
-    loop(0, T // W, lambda m: project(0, m))
-    done = 4
+    pump(4)
+    pass_on(3)
+    loop(0, NW, lambda m: project(0, m))
+    done = 5
     for h in range(HEADS):
-        attend(0, h)
-        if done < WST:
+        if h % 2 == 0 and done < LATE:
             pump(done)
             pass_on(done - 1)
             done += 1
-    have(3, 4)
-    attn_out(0, 0)
-    while done < WST:
+        attend(0, h)
+    while done < LATE:
         pump(done)
         pass_on(done - 1)
         done += 1
-    pass_on(WST - 1)
+    have(3, 4)
+    attn_out(0, 0)
+    pass_on(LATE - 1)
+    pump(LATE)
     loop(0, NCH, lambda m: norm_one(0, 0, m))
-    have(4, 8)
-    loop(0, NCH, lambda m: up_chunk(0, m))
+    pump(LATE + 1)
+    have(4, LATE)
+    for m in range(NW):
+        up_chunk(0, m)
+        pump(LATE + 2 + m)
     og_rows = pl.ds(t * B, B)
     og_mine, og_other = G.at[pl.ds(y * B, B)], G.at[pl.ds((1 - y) * B, B)]
     og_keep = pltpu.make_async_copy(og_mine, dattn.at[0, og_rows], lsem.at[0])
@@ -423,14 +452,15 @@
     og_keep.start()
     og_par.start()
     og_sib.start()
-    have(8, WST)
-    loop(0, NCH, lambda m: down_chunk(0, 1, m))
+    have(LATE, WST)
+    loop(0, NW, lambda m: down_chunk(0, 1, m))
 
     def next_layer(m):
-        norm_two(0, 1, m)
+        norm_two(0, 1, 2 * m)
+        norm_two(0, 1, 2 * m + 1)
         project(1, m)
 
-    loop(0, T // W, next_layer)
+    loop(0, NW, next_layer)
 
     attend_range(1, 0, HEADS)
     og_par.wait_recv()
@@ -439,21 +469,30 @@
     attn_out(1, 2)
 
     def feed_forward(m):
-        norm_one(1, 2, m)
+        norm_one(1, 2, 2 * m)
+        norm_one(1, 2, 2 * m + 1)
         up_chunk(1, m)
         down_chunk(1, 3, m)
 
-    loop(0, NCH, feed_forward)
+    loop(0, NW, feed_forward)
     loop(0, NCH, lambda m: norm_two(1, 3, m))
     out_keep = pltpu.make_async_copy(X.at[pl.ds(t * B, B)], out.at[y], lsem.at[1])
     out_par = remote(X.at[pl.ds(t2 * B, B)], out.at[y], fs.at[7], fr.at[7], par)
     out_keep.start()
     out_par.start()
     og_keep.wait()
+    for i in range(WST):
+        wy(i).wait_send()
+        wx(i).wait_send()
+        wz(i).wait_send()
+        if i >= LATE:
+            wd(i).wait_send()
+        else:
+            wf(i).wait_send()
     og_sib.wait_recv()
     og_fwd.wait_recv()
 
-    def ffn_back(l, k, m):
+    def norm_two_back(l, m):
         rows = chunk(m)
         dout = dattn[0, rows].astype(f32) if l == 1 else X[rows]
         scaled = zs[zrows(2 * l + 1, m)].astype(f32)
@@ -462,8 +501,11 @@
         acc[4:5] += col_sum(dout * scaled)
         acc[5:6] += col_sum(dout)
         Y[rows] = dr
-        drb = dr.astype(b16)
-        dffn[l, rows] = drb
+        dffn[l, rows] = dr.astype(b16)
+
+    def ffn_back(l, k, m):
+        rows = wide_chunk(m)
+        drb = dffn[l, rows]
         part = None
         for half in range(2):
             cols = pl.ds(half * D, D)
@@ -474,7 +516,7 @@
             acc[row : row + 1] += col_sum(dp.astype(f32))
             got = dot(dp, w[half, UP : UP + D], NT)
             part = got if part is None else part + got
-        xsend(k, m, part)
+        xsend_wide(k, m, part)
 
     def attn_out_back(l, k, m):
         rows = chunk(m)
@@ -513,19 +555,25 @@
 
     def project_back(l, k):
         def step(m):
-            tok = chunk(m)
+            tok = wide_chunk(m)
             part = dot(dqkv[l, 0 : 3 * A, tok], w[0, 0 : 3 * A], TN)
             part += dot(dqkv[l, 3 * A : 6 * A, tok], w[1, 0 : 3 * A], TN)
-            xsend(k, m, part)
-
-        loop(0, NCH, step)
+            xsend_wide(k, m, part)
+
+        loop(0, NW, step)
         ones = jnp.ones((8, T), b16)
         for half in range(2):
             sums = dot(ones, dqkv[l, half * 3 * A : (half + 1) * 3 * A], NT)
             row = 7 + 8 * half
             acc[row : row + 1, 0 : 3 * A] += sums[0:1]
 
-    loop(0, NCH, lambda m: ffn_back(1, 4, m))
+
+    def second_layer_back(m):
+        norm_two_back(1, 2 * m)
+        norm_two_back(1, 2 * m + 1)
+        ffn_back(1, 4, m)
+
+    loop(0, NW, second_layer_back)
     loop(0, NCH, lambda m: attn_out_back(1, 4, m))
     context_back(1)
     attend_back_range(1, 0, HEADS)
@@ -535,12 +583,14 @@
     out_par.wait_send()
     project_back(1, 5)
 
-    def first_layer(m):
-        rows = chunk(m)
-        X[rows] = Y[rows] + xget(5, m)
+    def first_layer_back(m):
+        for i in (2 * m, 2 * m + 1):
+            rows = chunk(i)
+            X[rows] = Y[rows] + xget(5, i)
+            norm_two_back(0, i)
         ffn_back(0, 6, m)
 
-    loop(0, NCH, first_layer)
+    loop(0, NW, first_layer_back)
 
     def both(ref, cols=slice(None)):
         value = ref[:, :, cols]
@@ -548,11 +598,13 @@
 
     FREE = T - 4 * A
 
-    def grad_down(half, dst, off=0):
+    def grad_down(half, dst, off=0, ready=None):
         dy = both(dffn)
         for i in reversed(range(D // 256)):
             left = both(act, slice(half * D + i * 256, half * D + (i + 1) * 256))
             dst[off + DN + i * 256 : off + DN + (i + 1) * 256] = dot(left, dy, TN).astype(b16)
+            if ready is not None:
+                ready((D // 256 - i) * 256 // R)
 
     def grad_up(half, dst, off=0):
         dy = both(dpre, slice(half * D, (half + 1) * D))
@@ -682,7 +734,16 @@
         for k in range(NP):
             axcopy(s, k).wait_recv()
 
-    stages = (stage_x, stage_z, stage_sum, stage_swap, stage_out)
+    def drain(s):
+        ycopy(s).wait_send()
+        gxcopy(s).wait_send()
+        for k in range(1, NP):
+            zcopy(s, k).wait_send()
+            azcopy(s, k).wait_send()
+        for k in range(NP):
+            axcopy(s, k).wait_send()
+
+    stages = (stage_x, stage_z, stage_sum, stage_swap, stage_out, drain)
 
     def run(i):
         for lag, stage in enumerate(stages):
@@ -691,9 +752,14 @@
                 continue
             stage(s)
 
-    grad_down(1, zs, FREE)
-    for s in range(YLOOK):
-        ystart(s)
+    begun = []
+
+    def begin(ready):
+        while len(begun) < min(ready, YLOOK):
+            ystart(len(begun))
+            begun.append(0)
+
+    grad_down(1, zs, FREE, begin)
     grad_up(1, zs, FREE)
     grad_down(0, G)
     loop(0, NCH, lambda m: attn_out_back(0, 6, m))
@@ -721,12 +787,13 @@
     gi_keep = pltpu.make_async_copy(xs.at[0, pl.ds(0, B)], gib_out.at[y], lsem.at[2])
     gi_par = remote(xs.at[0, pl.ds(B, B)], gib_out.at[y], fs.at[8], fr.at[8], par)
     gi_keep.start()
-    gi_par.start()
     grad_attn(0, G)
 
-    loop(4, D // R + 4, run)
+    run(4)
+    loop(5, D // R + 4, run)
     ocopies[0].start()
     loop(D // R + 4, NS, run)
+    gi_par.start()
     for i in range(NS, NS + 2):
         run(i)
     sm_y.wait_recv()
@@ -768,22 +835,7 @@
     out_par.wait_recv()
     gi_par.wait_recv()
     gi_keep.wait()
-    for i in range(WST):
-        wy(i).wait_send()
-        wx(i).wait_send()
-        wz(i).wait_send()
-        wf(i).wait_send()
-
-    def drain(s):
-        ycopy(s).wait_send()
-        gxcopy(s).wait_send()
-        for k in range(1, NP):
-            zcopy(s, k).wait_send()
-            azcopy(s, k).wait_send()
-        for k in range(NP):
-            axcopy(s, k).wait_send()
-
-    loop(0, NS, drain)
+    drain(NS - 1)
     for copy in ocopies:
         copy.wait()
 
@@ -853,7 +905,7 @@
     while nz % (2 * NP) == 0 and HR % (32 * NP) == 0:
         NP *= 2
     NH = nz // NP
-    C = T // 2
+    C = T // 4
     NCH = T // C
     NS = TOT // R
     Q = HR // NP
@@ -915,6 +967,8 @@
         DMA((9,)),
         DMA((12,)),
         DMA((12,)),
+        DMA((TOT // A,)),
+        DMA((TOT // A,)),
         DMA((TOT // A,)),
         DMA((TOT // A,)),
         DMA((TOT // A,)),

time: 204 us -> 192 us (0.941)
  Pallas kernels: 203 us -> 191 us
    pallas_call x1, Pallas kernels: 197 us -> 185 us  [shards(): pl.pallas_call(functools.partial(whole_step, cfg), out_shape=(jax.ShapeDt...]
where the time goes in v1:
time: 192 us
  Pallas kernels  191 us (99%)
    pallas_call x1, Pallas kernels, shards(): pl.pallas_call(functools.partial(whole_step, cfg), out_shape=(jax.ShapeDt...  185 us
    pallas_call x1, Pallas kernels, shards(): pl.pallas_call(widen, out_shape=tuple((jax.ShapeDtypeStruct(v.shape, f32)...  6.3 us

profile of v1, /device:TPU:0, one launch (start us, length us, event | category | flops | bytes accessed | tf_op | source)
XLA Modules:
  0.0 192.2 jit_solution(12228676567653150989)
XLA Ops:
  0.7 185.1 %shard_map.305 = (f32[2,128,768]{2,1,0:T(8,128)}, bf16[2,128,768]{2,1,0:T(8,128)(2,1)}, bf16[192,768]{1,0:T(8,128)(2,1)}, bf16[192,768]{1,0:T(8,128)(2,1)}, bf16...) custom-call(s32[2]{0:T(128)} %len_ref.1, ...), custom_call_target="tpu_custom_call" | custom-call | tf_op jit(solution)/shard_map/pallas_call | solution.py:1001
  185.7 6.3 %shard_map.306 = (f32[768,768]{1,0:T(8,128)}, f32[768,768]{1,0:T(8,128)}, f32[192,768]{1,0:T(8,128)}, f32[192,768]{1,0:T(8,128)}, f32[192,768]{1,0:T(8,128)}, /*...) custom-call(bf16[768,768]{1,0:T(8,128)(2,1)} %get-tuple-element.43.r, ...), custom_call_target="tpu_custom_call" | custom-call | tf_op jit(solution)/shard_map/pallas_call | solution.py:1033

commit v2 on v1

--- a/solution.py
+++ b/solution.py
@@ -346,7 +346,10 @@
 
     def head_rows(h, part):
         base = (h // NHH) * (3 * A) + part * A + (h % NHH) * HEAD
-        return pl.ds(pl.multiple_of(base, HEAD), HEAD)
+        return pl.ds(base if isinstance(h, int) else pl.multiple_of(base, HEAD), HEAD)
+
+    def ctx_rows(h):
+        return pl.ds(h * HEAD if isinstance(h, int) else pl.multiple_of(h * HEAD, HEAD), HEAD)
 
     def attend(l, h):
         counted = lax.broadcasted_iota(jnp.int32, (T, T), 0) < length
@@ -359,10 +362,14 @@
         ex[l, h] = eb
         inv[l, h] = one
         got = dot(qkv[l, head_rows(h, 2)], eb, NN) * one
-        ctx[l, pl.ds(pl.multiple_of(h * HEAD, HEAD), HEAD)] = got.astype(b16)
+        ctx[l, ctx_rows(h)] = got.astype(b16)
 
     def attend_range(l, lo, hi):
-        loop(lo, hi, lambda h: attend(l, h))
+        if l == 0:
+            loop(lo, hi, lambda h: attend(l, h))
+        else:
+            for h in range(lo, hi):
+                attend(l, h)
 
     def attn_out(l, k):
         def step(m):
@@ -424,12 +431,12 @@
     pass_on(3)
     loop(0, NW, lambda m: project(0, m))
     done = 5
-    for h in range(HEADS):
-        if h % 2 == 0 and done < LATE:
+    for h in range(0, HEADS, 2):
+        if done < LATE:
             pump(done)
             pass_on(done - 1)
             done += 1
-        attend(0, h)
+        attend_range(0, h, min(h + 2, HEADS))
     while done < LATE:
         pump(done)
         pass_on(done - 1)
@@ -539,7 +546,7 @@
                 dct[h * HEAD : (h + 1) * HEAD] = scaled_rows.astype(b16)
 
     def attend_back(l, h):
-        mine = pl.ds(pl.multiple_of(h * HEAD, HEAD), HEAD)
+        mine = ctx_rows(h)
         dc = dct[mine]
         dprobs = dot(qkv[l, head_rows(h, 2)], dc, TN)
         eb = ex[l, h]
@@ -551,7 +558,11 @@
         dqkv[l, head_rows(h, 1)] = dot(qkv[l, head_rows(h, 0)], ds, NT).astype(b16)
 
     def attend_back_range(l, lo, hi):
-        loop(lo, hi, lambda h: attend_back(l, h))
+        if l == 0:
+            loop(lo, hi, lambda h: attend_back(l, h))
+        else:
+            for h in range(lo, hi):
+                attend_back(l, h)
 
     def project_back(l, k):
         def step(m):
@@ -592,33 +603,43 @@
 
     loop(0, NW, first_layer_back)
 
-    def both(ref, cols=slice(None)):
-        value = ref[:, :, cols]
-        return value.reshape(2 * value.shape[1], value.shape[2])
-
     FREE = T - 4 * A
 
-    def grad_down(half, dst, off=0, ready=None):
-        dy = both(dffn)
-        for i in reversed(range(D // 256)):
-            left = both(act, slice(half * D + i * 256, half * D + (i + 1) * 256))
-            dst[off + DN + i * 256 : off + DN + (i + 1) * 256] = dot(left, dy, TN).astype(b16)
-            if ready is not None:
-                ready((D // 256 - i) * 256 // R)
+    GB = D // 256
+
+    def grad_down(half, dst, off=0, lo=0, hi=GB):
+        def step(j):
+            at = pl.multiple_of((GB - 1 - j) * 256, 256)
+            got = None
+            for l in range(2):
+                one = dot(act[l, :, pl.ds(half * D + at, 256)], dffn[l], TN)
+                got = one if got is None else got + one
+            dst[pl.ds(pl.multiple_of(off + DN + at, 256), 256)] = got.astype(b16)
+
+        loop(lo, hi, step)
 
     def grad_up(half, dst, off=0):
-        dy = both(dpre, slice(half * D, (half + 1) * D))
-        for i in reversed(range(D // 256)):
-            left = both(yb, slice(i * 256, (i + 1) * 256))
-            dst[off + UP + i * 256 : off + UP + (i + 1) * 256] = dot(left, dy, TN).astype(b16)
+        def step(j):
+            at = pl.multiple_of((GB - 1 - j) * 256, 256)
+            got = None
+            for l in range(2):
+                one = dot(yb[l, :, pl.ds(at, 256)], dpre[l, :, half * D : (half + 1) * D], TN)
+                got = one if got is None else got + one
+            dst[pl.ds(pl.multiple_of(off + UP + at, 256), 256)] = got.astype(b16)
+
+        loop(0, GB, step)
 
     def grad_attn(half, dst):
         rows = slice(half * A, (half + 1) * A)
         got = dot(ctx[0, rows], dattn[0], NN) + dot(ctx[1, rows], dattn[1], NN)
         dst[3 * A : 4 * A] = got.astype(b16)
-        rows = slice(half * 3 * A, (half + 1) * 3 * A)
-        got = dot(dqkv[0, rows], hb[0], NN) + dot(dqkv[1, rows], hb[1], NN)
-        dst[0 : 3 * A] = got.astype(b16)
+
+        def step(i):
+            rows = pl.ds(pl.multiple_of(half * 3 * A + i * A, A), A)
+            got = dot(dqkv[0, rows], hb[0], NN) + dot(dqkv[1, rows], hb[1], NN)
+            dst[pl.ds(pl.multiple_of(i * A, A), A)] = got.astype(b16)
+
+        loop(0, 3, step)
 
     def top_of(s):
         return pl.multiple_of(TOT - (s + 1) * R, R)
@@ -752,14 +773,13 @@
                 continue
             stage(s)
 
-    begun = []
-
-    def begin(ready):
-        while len(begun) < min(ready, YLOOK):
-            ystart(len(begun))
-            begun.append(0)
-
-    grad_down(1, zs, FREE, begin)
+    first_ready = min(256 // R, YLOOK)
+    grad_down(1, zs, FREE, 0, 1)
+    for s in range(first_ready):
+        ystart(s)
+    grad_down(1, zs, FREE, 1, GB)
+    for s in range(first_ready, YLOOK):
+        ystart(s)
     grad_up(1, zs, FREE)
     grad_down(0, G)
     loop(0, NCH, lambda m: attn_out_back(0, 6, m))

time: 192 us -> 190 us (0.990)
  Pallas kernels: 191 us -> 189 us
    pallas_call x1, Pallas kernels: 185 us -> 183 us  [shards(): pl.pallas_call(functools.partial(whole_step, cfg), out_shape=(jax.ShapeDt...]
where the time goes in v2:
time: 190 us
  Pallas kernels  189 us (99%)
    pallas_call x1, Pallas kernels, shards(): pl.pallas_call(functools.partial(whole_step, cfg), out_shape=(jax.ShapeDt...  183 us
    pallas_call x1, Pallas kernels, shards(): pl.pallas_call(widen, out_shape=tuple((jax.ShapeDtypeStruct(v.shape, f32)...  6.3 us

profile of v2, /device:TPU:0, one launch (start us, length us, event | category | flops | bytes accessed | tf_op | source)
XLA Modules:
  0.0 189.8 jit_solution(324281005504009856)
XLA Ops:
  0.7 182.6 %shard_map.305 = (f32[2,128,768]{2,1,0:T(8,128)}, bf16[2,128,768]{2,1,0:T(8,128)(2,1)}, bf16[192,768]{1,0:T(8,128)(2,1)}, bf16[192,768]{1,0:T(8,128)(2,1)}, bf16...) custom-call(s32[2]{0:T(128)} %len_ref.1, ...), custom_call_target="tpu_custom_call" | custom-call | tf_op jit(solution)/shard_map/pallas_call | solution.py:1021
  183.3 6.3 %shard_map.306 = (f32[768,768]{1,0:T(8,128)}, f32[768,768]{1,0:T(8,128)}, f32[192,768]{1,0:T(8,128)}, f32[192,768]{1,0:T(8,128)}, f32[192,768]{1,0:T(8,128)}, /*...) custom-call(bf16[768,768]{1,0:T(8,128)(2,1)} %get-tuple-element.43.r, ...), custom_call_target="tpu_custom_call" | custom-call | tf_op jit(solution)/shard_map/pallas_call | solution.py:1053

commit v3 on v2

--- a/solution.py
+++ b/solution.py
@@ -49,15 +49,15 @@
     wo,
     wu,
     wd,
-    bu,
-    bq,
-    bv,
-    b_out,
-    gain1,
-    shift1,
-    b_down,
-    gain2,
-    shift2,
+    bu_in,
+    bq_in,
+    bv_in,
+    b_out_in,
+    gain1_in,
+    shift1_in,
+    b_down_in,
+    gain2_in,
+    shift2_in,
     out,
     gib_out,
     gq_out,
@@ -101,6 +101,16 @@
     zr,
     hr,
     F,
+    bu,
+    bq,
+    bv,
+    b_out,
+    gain1,
+    shift1,
+    b_down,
+    gain2,
+    shift2,
+    vsem,
     lsem,
     fs,
     fr,
@@ -183,6 +193,24 @@
             device_id_type=MESH,
         )
 
+    vectors = [
+        pltpu.make_async_copy(src, dst, vsem.at[i])
+        for i, (src, dst) in enumerate(
+            (
+                (bu_in, bu),
+                (bq_in, bq),
+                (bv_in, bv),
+                (b_out_in, b_out),
+                (gain1_in, gain1),
+                (shift1_in, shift1),
+                (b_down_in, b_down),
+                (gain2_in, gain2),
+                (shift2_in, shift2),
+            )
+        )
+    ]
+    for copy in vectors:
+        copy.start()
     local = [
         pltpu.make_async_copy(hid.at[y], hb.at[0, pl.ds(t * B, B)], lsem.at[0]),
         pltpu.make_async_copy(wo, w.at[0, pl.ds(3 * A, A)], lsem.at[1]),
@@ -205,6 +233,8 @@
 
     hid_sib = remote(hid.at[y], hb.at[0, pl.ds(t * B, B)], fs.at[0], fr.at[0], sib)
     hid_par = remote(hid.at[1 - y], hb.at[0, pl.ds(t * B, B)], fs.at[1], fr.at[1], par)
+    for copy in vectors:
+        copy.wait()
     bias_par = [
         remote(mine, theirs, fs.at[9 + i], fr.at[9 + i], par)
         for i, (mine, theirs) in enumerate(((bu, bur), (bq, bqr), (bv, bvr)))
@@ -846,15 +876,19 @@
         for k, copy in enumerate(sm_h):
             copy.wait()
             total += smr[NP + 1 + k]
-    sm_out[...] = total
-
-    for copy in (hid_sib, hid_par, *bias_par, hid_fwd, gi_par, sm_y, sm_x):
+    sm_x.wait_send()
+    sm[0] = total
+    small_keep = pltpu.make_async_copy(sm.at[0], sm_out, vsem.at[0])
+    small_keep.start()
+
+    for copy in (hid_sib, hid_par, *bias_par, hid_fwd, gi_par, sm_y):
         copy.wait_send()
     for copy in sm_z:
         copy.wait_send()
     out_par.wait_recv()
     gi_par.wait_recv()
     gi_keep.wait()
+    small_keep.wait()
     drain(NS - 1)
     for copy in ocopies:
         copy.wait()
@@ -867,7 +901,9 @@
     wide, result_out, vectors = refs[:names], refs[names], refs[names + 1 : names + 10]
     refs = refs[names + 10 :]
     narrow, broad = refs[:names], refs[names : 2 * names]
-    through, isem, osem = refs[2 * names :]
+    through, sums, *held, isem, osem = refs[2 * names :]
+    get_sums = pltpu.make_async_copy(small, sums, isem.at[names + 1])
+    get_sums.start()
     loads = [pltpu.make_async_copy(big[i], narrow[i], isem.at[i]) for i in range(names)]
     stores = [pltpu.make_async_copy(broad[i], wide[i], osem.at[i]) for i in range(names)]
     keep_in = pltpu.make_async_copy(result, through, isem.at[names])
@@ -875,20 +911,24 @@
     for copy in loads:
         copy.start()
     keep_in.start()
-    for i, ref in enumerate(vectors):
+    get_sums.wait()
+    small_out = []
+    for i, (ref, dst) in enumerate(zip(held, vectors)):
         if i < 7:
-            ref[...] = small[i, :]
+            ref[...] = sums[i, :]
         else:
             rows = ref.shape[0]
             at = (i - 7) * 2 * rows
-            ref[...] = small[7, at : at + rows]
+            ref[...] = sums[7, at : at + rows]
+        small_out.append(pltpu.make_async_copy(ref, dst, osem.at[names + 1 + i]))
+        small_out[-1].start()
     for load, store, i in zip(loads, stores, range(names)):
         load.wait()
         broad[i][...] = narrow[i][...].astype(f32)
         store.start()
     keep_in.wait()
     keep.start()
-    for copy in stores:
+    for copy in stores + small_out:
         copy.wait()
     keep.wait()
 
@@ -984,6 +1024,8 @@
         V((NS, NPx, Q, D), b16),
         V((2, NHx, Q, D), b16),
         V((TOT, D), b16),
+        *[V(value.shape, f32) for value in rows],
+        DMA((9,)),
         DMA((9,)),
         DMA((12,)),
         DMA((12,)),
@@ -1016,7 +1058,6 @@
         DMA((NP + NH,)),
     ]
     anywhere = pl.BlockSpec(memory_space=pl.ANY)
-    vmem = pl.BlockSpec(memory_space=pltpu.VMEM)
     smem = pl.BlockSpec(memory_space=pltpu.SMEM)
     result, gib, gq, gk, gv, go, gu, gd, small = pl.pallas_call(
         functools.partial(whole_step, cfg),
@@ -1031,8 +1072,8 @@
             jax.ShapeDtypeStruct((D, D), b16),
             jax.ShapeDtypeStruct((8, D), f32),
         ),
-        in_specs=[smem] + [anywhere] * 8 + [vmem] * 9,
-        out_specs=(anywhere,) * 8 + (vmem,),
+        in_specs=[smem] + [anywhere] * 17,
+        out_specs=(anywhere,) * 9,
         scratch_shapes=scratch,
         compiler_params=pltpu.CompilerParams(
             collective_id=0, has_side_effects=True, vmem_limit_bytes=64 * 2**20
@@ -1055,11 +1096,14 @@
         out_shape=tuple(jax.ShapeDtypeStruct(v.shape, f32) for v in bigs + (result,))
         + (jax.ShapeDtypeStruct((D,), f32),) * 7
         + (jax.ShapeDtypeStruct((A,), f32),) * 2,
-        in_specs=[anywhere] * 8 + [vmem],
-        out_specs=(anywhere,) * 8 + (vmem,) * 9,
+        in_specs=[anywhere] * 9,
+        out_specs=(anywhere,) * 17,
         scratch_shapes=[V(v.shape, b16) for v in bigs]
         + [V(v.shape, f32) for v in bigs]
-        + [V(result.shape, f32), DMA((8,)), DMA((8,))],
+        + [V(result.shape, f32), V((8, D), f32)]
+        + [V((D,), f32)] * 7
+        + [V((A,), f32)] * 2
+        + [DMA((9,)), DMA((17,))],
         compiler_params=pltpu.CompilerParams(vmem_limit_bytes=64 * 2**20),
     )(*bigs, result, small)
     db_out, dgain1, dshift1, db_down, dgain2, dshift2, db_up, db_query, db_value = vectors

time: 190 us -> 189 us (level)
  no operation moved by 1% of the time
where the time goes in v3:
time: 189 us; the launch traced here: 188 us
  Pallas kernels  188 us (99%)
    pallas_call x1, Pallas kernels, shards(): pl.pallas_call(functools.partial(whole_step, cfg), out_shape=(jax.ShapeDt...  183 us
    pallas_call x1, Pallas kernels, shards(): pl.pallas_call(widen, out_shape=tuple((jax.ShapeDtypeStruct(v.shape, f32)...  5.06 us

profile of v3, /device:TPU:0, one launch (start us, length us, event | category | flops | bytes accessed | tf_op | source)
XLA Modules:
  0.0 188.4 jit_solution(10534258457616778842)
XLA Ops:
  0.7 182.5 %shard_map.305 = (f32[2,128,768]{2,1,0:T(8,128)}, bf16[2,128,768]{2,1,0:T(8,128)(2,1)}, bf16[192,768]{1,0:T(8,128)(2,1)}, bf16[192,768]{1,0:T(8,128)(2,1)}, bf16...) custom-call(s32[2]{0:T(128)} %len_ref.1, ...), custom_call_target="tpu_custom_call" | custom-call | tf_op jit(solution)/shard_map/pallas_call | solution.py:1062
  183.2 5.1 %shard_map.306 = (f32[768,768]{1,0:T(8,128)}, f32[768,768]{1,0:T(8,128)}, f32[192,768]{1,0:T(8,128)}, f32[192,768]{1,0:T(8,128)}, f32[192,768]{1,0:T(8,128)}, /*...) custom-call(bf16[768,768]{1,0:T(8,128)(2,1)} %get-tuple-element.43.r, ...), custom_call_target="tpu_custom_call" | custom-call | tf_op jit(solution)/shard_map/pallas_call | solution.py:1094
